TPU v7x, 32 devices: a whole 2x2x4 slice. The times are simulated.
32 devices in a mesh: layer: 2 (over y), basis: 4 (over z), tok: 4 (over x, core).
Axes of the slice: x: 2, y: 2, z: 4, core: 2. Of those that a mesh axis runs over, the one named last changes fastest.
Arguments:
- activations: bfloat16 [2048, 8192], P(('layer', 'tok'), 'basis'), parts along dimension 0, may hold values from -16 to 16
- gradients: bfloat16 [2048, 8192], P(('layer', 'tok'), 'basis'), parts along dimension 0, may hold values from -16 to 16
- input_basis: bfloat16 [16384, 8192], P(('layer', 'tok'), 'basis'), parts along dimension 0, may hold values from -0.0625 to 0.0625
- output_basis: bfloat16 [16384, 8192], P(('layer', 'tok'), 'basis'), parts along dimension 0, may hold values from -0.0625 to 0.0625
Outputs:
- eigenvalues: float32 [16384, 8192], P(('layer', 'tok'), 'basis'), parts along dimension 0
There are 2 independent parts, one for each index of `layer`. A program takes and returns all parts, laid end to end along the dimension named above; each array names one. Nothing has to cross between parts.
All inputs are finite; a program needn't handle non-finite values.
Results may differ from a plain program's by a relative error of at most 0.00039.
Values may be sent and summed in bfloat16 or wider, within the bound.
A program may use at most 256 MiB of HBM per device.

v0:
```python
import jax
import jax.numpy as jnp
from jax import lax
from jax.sharding import PartitionSpec as P


def on_device(activations, gradients, input_basis, output_basis):
    full_acts, full_grads = (
        lax.all_gather(activations, "basis", axis=1, tiled=True),
        lax.all_gather(gradients, "basis", axis=1, tiled=True),
    )
    tok_rows = full_acts.shape[0]
    projected_in = jnp.dot(
        full_acts,
        lax.all_gather(input_basis, "tok", axis=0, tiled=True),
        preferred_element_type=jnp.float32,
    )
    projected_out = jnp.dot(
        full_grads,
        lax.all_gather(output_basis, "tok", axis=0, tiled=True),
        preferred_element_type=jnp.float32,
    )
    squared_in = (projected_in * projected_in).astype(jnp.bfloat16)
    squared_out = (projected_out * projected_out).astype(jnp.bfloat16)
    every_in = lax.all_gather(squared_in, "basis", axis=1, tiled=True)
    total_tokens = tok_rows * lax.axis_size("tok")
    summed = lax.psum_scatter(
        lax.dot_general(
            every_in, squared_out, (((0,), (0,)), ((), ())), preferred_element_type=jnp.float32
        ),
        "tok",
        scatter_dimension=0,
        tiled=True,
    )
    return summed / total_tokens


def solution(mesh):
    return jax.shard_map(
        on_device,
        mesh=mesh,
        in_specs=(
            P(("layer", "tok"), "basis"),
            P(("layer", "tok"), "basis"),
            P(("layer", "tok"), "basis"),
            P(("layer", "tok"), "basis"),
        ),
        out_specs=P(("layer", "tok"), "basis"),
        check_vma=False,
    )
```

profile of v0, /device:TPU:0, one launch (start us, length us, event | category | flops | bytes accessed | tf_op | source)
XLA Modules:
  0.0 1155.4 jit_solution(15035272221816858705)
XLA Ops:
  6.5 0.0 all-gather.6.cloned.1.call-start
  6.5 0.7 all-gather.6.cloned.1.call-update
  7.3 0.0 all-gather.8.cloned.1.call-start
  7.3 0.7 all-gather.8.cloned.1.call-update
  8.0 0.0 all-gather.12.cloned.1.call-start
  8.1 0.7 all-gather.12.cloned.1.call-update
  8.7 0.0 all-gather.14.cloned.1.call-start
  8.8 0.5 all-gather.14.cloned.1.call-update
  9.3 0.0 all-gather.10.cloned.1.call-start
  9.4 83.1 %all-gather.6.cloned.1.call-done = bf16[256,8192]{1,0:T(8,128)(2,1)} async-done(((bf16[256,2048]{1,0:T(8,128)(2,1)}), bf16[256,8192]{1,0:T(8,128)(2,1)}) %all-gather.6.cloned.1.call-update) | async-done | bytes 4194320 | tf_op jit(solution)/shard_map/all_gather | solution.py:9
  92.4 201.6 %all-gather.8.cloned.1.call-done = bf16[8192,2048]{1,0:T(8,128)(2,1)} async-done(((bf16[2048,2048]{1,0:T(8,128)(2,1)}), bf16[8192,2048]{1,0:T(8,128)(2,1)}) %all-gather.8.cloned.1.call-update) | async-done | bytes 33554448 | tf_op jit(solution)/shard_map/all_gather | solution.py:15
  294.1 18.2 %fusion = bf16[256,2048]{1,0:T(8,128)(2,1)} fusion(bf16[256,8192]{1,0:T(8,128)(2,1)} %all-gather.6.cloned.1.call-done, bf16[8192,2048]{1,0:T(8,128)(2,1)} %all-gather.8.cloned.1.call-done), kind=kOutput, calls=%fused_computation.3 | convolution fusion | flops 8590983168 | bytes 38797312 | tf_op jit(solution)/shard_map/dot_general | solution.py:13
  312.3 0.0 all-gather.10.cloned.1.call-update
  312.3 0.0 reduce-scatter.4.cloned.1.call-start
  312.4 64.1 %all-gather.12.cloned.1.call-done = bf16[256,8192]{1,0:T(8,128)(2,1)} async-done(((bf16[256,2048]{1,0:T(8,128)(2,1)}), bf16[256,8192]{1,0:T(8,128)(2,1)}) %all-gather.12.cloned.1.call-update) | async-done | bytes 4194320 | tf_op jit(solution)/shard_map/all_gather | solution.py:10
  376.4 201.5 %all-gather.14.cloned.1.call-done = bf16[8192,2048]{1,0:T(8,128)(2,1)} async-done(((bf16[2048,2048]{1,0:T(8,128)(2,1)}), bf16[8192,2048]{1,0:T(8,128)(2,1)}) %all-gather.14.cloned.1.call-update) | async-done | bytes 33554448 | tf_op jit(solution)/shard_map/all_gather | solution.py:20
  578.0 17.3 %fusion.1 = bf16[256,2048]{1,0:T(8,128)(2,1)S(1)} fusion(bf16[256,8192]{1,0:T(8,128)(2,1)} %all-gather.12.cloned.1.call-done, bf16[8192,2048]{1,0:T(8,128)(2,1)} %all-gather.14.cloned.1.call-done), kind=kOutput, calls=%fused_computation.4 | convolution fusion | flops 8590983168 | bytes 38797312 | tf_op jit(solution)/shard_map/dot_general | solution.py:18
  595.3 64.9 %all-gather.10.cloned.1.call-done = bf16[256,8192]{1,0:T(8,128)(2,1)} async-done(((bf16[256,2048]{1,0:T(8,128)(2,1)}), bf16[256,8192]{1,0:T(8,128)(2,1)}) %all-gather.10.cloned.1.call-update) | async-done | bytes 4194320 | tf_op jit(solution)/shard_map/all_gather | solution.py:25
  660.2 25.3 %fusion.2 = f32[8192,2048]{1,0:T(8,128)} fusion(bf16[256,8192]{1,0:T(8,128)(2,1)} %all-gather.10.cloned.1.call-done, bf16[256,2048]{1,0:T(8,128)(2,1)S(1)} %fusion.1), kind=kOutput, calls=%fused_computation.5 | convolution fusion | flops 8589934592 | bytes 72351744 | tf_op jit(solution)/shard_map/dot_general | solution.py:28
  685.5 0.0 reduce-scatter.4.cloned.1.call-update
  685.5 451.1 %reduce-scatter.4.cloned.1.call-done = f32[2048,2048]{1,0:T(8,128)} async-done(((f32[8192,2048]{1,0:T(8,128)}), f32[2048,2048]{1,0:T(8,128)}) %reduce-scatter.4.cloned.1.call-update) | async-done | bytes 16777232
  1136.6 12.0 %broadcast_multiply_fusion = f32[2048,2048]{1,0:T(8,128)} fusion(f32[2048,2048]{1,0:T(8,128)} %reduce-scatter.4.cloned.1.call-done), kind=kLoop, calls=%fused_computation | loop fusion | flops 4194304 | bytes 33554432 | tf_op jit(solution)/shard_map/div | solution.py:35
Async XLA Ops:
  6.5 85.9 %all-gather.6.cloned.1.call-start = ((), (), s32[]{:S(2)}) async-start(), calls=%async_computation.1 | async-start | bytes 5242880 | tf_op jit(solution)/shard_map/all_gather | solution.py:9
  7.3 286.8 %all-gather.8.cloned.1.call-start = ((), (), s32[]{:S(2)}) async-start(), calls=%async_computation.2 | async-start | bytes 41943040 | tf_op jit(solution)/shard_map/all_gather | solution.py:15
  8.0 368.4 %all-gather.12.cloned.1.call-start = ((), (), s32[]{:S(2)}) async-start(), calls=%async_computation.4 | async-start | bytes 5242880 | tf_op jit(solution)/shard_map/all_gather | solution.py:10
  8.7 569.2 %all-gather.14.cloned.1.call-start = ((), (), s32[]{:S(2)}) async-start(), calls=%async_computation.5 | async-start | bytes 41943040 | tf_op jit(solution)/shard_map/all_gather | solution.py:20
  9.3 650.9 %all-gather.10.cloned.1.call-start = ((), (), s32[]{:S(2)}) async-start(), calls=%async_computation.3 | async-start | bytes 5242880 | tf_op jit(solution)/shard_map/all_gather | solution.py:25
  312.3 824.3 %reduce-scatter.4.cloned.1.call-start = ((), (), s32[]{:S(2)}) async-start(), calls=%async_computation.6 | async-start | bytes 83886080
Sparse Core Ops, SparseCore 0:
  8.9 83.4 all-gather.5
  94.0 200.0 all-gather.7
  295.6 80.7 all-gather.11
  377.9 200.0 all-gather.13
  579.4 80.7 all-gather.9
  685.7 450.9 reduce-scatter.3
where the time goes:
time: 1160 us
  waiting for transfers between devices  1070 us (92%)
  matrix products  60.9 us (5%)
  between operations  13.5 us (1%)
  other arithmetic  12 us (1%)
    unnamed x7, waiting for transfers between devices  454 us
    all_gather x1, waiting for transfers between devices, on_device(): lax.all_gather(input_basis, 'tok', axis=0, tiled=True)  202 us
    all_gather x1, waiting for transfers between devices, on_device(): lax.all_gather(output_basis, 'tok', axis=0, tiled=True)  202 us
    all_gather x1, waiting for transfers between devices, on_device(): lax.all_gather(activations, 'basis', axis=1, tiled=True)  83.1 us
    all_gather x1, waiting for transfers between devices, on_device(): every_in = lax.all_gather(squared_in, 'basis', axis=1, tiled=True)  64.9 us
    all_gather x1, waiting for transfers between devices, on_device(): lax.all_gather(gradients, 'basis', axis=1, tiled=True)  64.1 us
    dot_general x1, matrix products, on_device(): lax.dot_general(every_in, squared_out, (((0,), (0,)), ((), ())), preferre...  25.3 us
  transfers between devices with their start and end apart: 6, of which 6 were waited for; matrix products, arithmetic and copies ran while one was open for 3% of the time, Pallas kernels for 0%

commit v1 on v0

v1 whole, which is shorter than its diff:
```python
import jax
import jax.numpy as jnp
from jax import lax
from jax.sharding import PartitionSpec as P


def all_tokens_of_own_block(block):
    n_tok, n_basis = lax.axis_size("tok"), lax.axis_size("basis")
    if n_tok == n_basis:
        swaps = [(b * n_tok + t, t * n_tok + b) for b in range(n_basis) for t in range(n_tok)]
        swapped = lax.ppermute(block, ("basis", "tok"), swaps)
        return lax.all_gather(swapped, "basis", axis=0, tiled=True)
    full = lax.all_gather(block, "basis", axis=1, tiled=True)
    return lax.all_to_all(full, "tok", split_axis=1, concat_axis=0, tiled=True)


def project(block, basis_block):
    partial = jnp.dot(
        all_tokens_of_own_block(block), basis_block, preferred_element_type=jnp.float32
    )
    return lax.psum_scatter(partial, "tok", scatter_dimension=0, tiled=True)


def on_device(activations, gradients, input_basis, output_basis):
    tok_rows = activations.shape[0]
    projected_in = project(activations, input_basis)
    squared_in = (projected_in * projected_in).astype(jnp.bfloat16)
    projected_out = project(gradients, output_basis)
    squared_out = (projected_out * projected_out).astype(jnp.bfloat16)
    every_in = all_tokens_of_own_block(squared_in)
    every_out = lax.all_gather(squared_out, "tok", axis=0, tiled=True)
    total_tokens = tok_rows * lax.axis_size("tok")
    summed = lax.dot_general(
        every_in, every_out, (((0,), (0,)), ((), ())), preferred_element_type=jnp.float32
    )
    return summed / total_tokens


def solution(mesh):
    spec = P(("layer", "tok"), "basis")
    return jax.shard_map(
        on_device, mesh=mesh, in_specs=(spec,) * 4, out_specs=spec, check_vma=False
    )
```

time: 1160 us -> 569 us (0.49)
  waiting for transfers between devices: 1070 us -> 499 us
  matrix products: 60.9 us -> 44.8 us
    unnamed x7 -> x6, waiting for transfers between devices: 454 us -> 0.1 us
    all_gather x5 -> x4, waiting for transfers between devices: 615 us -> 369 us  [the longest x3 319 us: all_tokens_of_own_block(): return lax.all_gather(swapped, 'basis', axis=0, tiled=True)]
    reduce_scatter x0 -> x2, waiting for transfers between devices: none -> 129 us  [project(): return lax.psum_scatter(partial, 'tok', scatter_dimension=0, tiled=True)]
    dot_general x3, matrix products: 60.9 us -> 44.8 us  [the longest x2 29.4 us: project(): jnp.dot(all_tokens_of_own_block(block), basis_block, preferred_element_ty...]
    div x1 -> x0, other arithmetic: 12 us -> none  [on_device(): return summed / total_tokens]
  transfers between devices with their start and end apart: 6 -> 9, of which waited for: 6 -> 6; matrix products, arithmetic and copies ran while one was open for 3% -> 6% of each run, Pallas kernels for 0% -> 0%
where the time goes in v1:
time: 569 us
  waiting for transfers between devices  499 us (88%)
  matrix products  44.8 us (8%)
  between operations  13.5 us (2%)
    all_gather x3, waiting for transfers between devices, all_tokens_of_own_block(): return lax.all_gather(swapped, 'basis', axis=0, tiled=True)  319 us
    reduce_scatter x2, waiting for transfers between devices, project(): return lax.psum_scatter(partial, 'tok', scatter_dimension=0, tiled=True)  129 us
    all_gather x1, waiting for transfers between devices, on_device(): every_out = lax.all_gather(squared_out, 'tok', axis=0, tiled=True)  50.1 us
    dot_general x2, matrix products, project(): jnp.dot(all_tokens_of_own_block(block), basis_block, preferred_element_ty...  29.4 us
    dot_general x1, matrix products, on_device(): lax.dot_general(every_in, every_out, (((0,), (0,)), ((), ())), preferred_...  15.4 us
  transfers between devices with their start and end apart: 9, of which 6 were waited for; matrix products, arithmetic and copies ran while one was open for 6% of the time, Pallas kernels for 0%

profile of v1, /device:TPU:0, one launch (start us, length us, event | category | flops | bytes accessed | tf_op | source)
XLA Modules:
  0.0 569.1 jit_solution(6837975107625153471)
XLA Ops:
  6.5 0.0 all-gather.9.cloned.1.call-start
  6.5 1.9 collective-permute-start.2
  8.4 0.0 collective-permute-done.2
  8.4 0.0 copy-start
  8.4 1.0 copy-done
  9.4 0.0 all-gather.9.cloned.1.call-update
  9.4 0.0 all-gather.5.cloned.1.call-start
  9.5 1.9 collective-permute-start
  11.4 0.0 collective-permute-done
  11.4 0.0 copy-start.1
  11.4 1.0 copy-done.1
  12.3 0.0 all-gather.5.cloned.1.call-update
  12.3 0.0 reduce-scatter.5.cloned.1.call-start
  12.4 166.6 %all-gather.9.cloned.1.call-done = bf16[1024,2048]{1,0:T(8,128)(2,1)} async-done(((bf16[256,2048]{1,0:T(8,128)(2,1)}), bf16[1024,2048]{1,0:T(8,128)(2,1)}) %all-gather.9.cloned.1.call-update) | async-done | bytes 4194320 | tf_op jit(solution)/shard_map/all_gather | solution.py:12
  179.0 14.6 %fusion.1 = f32[1024,2048]{1,0:T(8,128)} fusion(bf16[1024,2048]{1,0:T(8,128)(2,1)} %all-gather.9.cloned.1.call-done, bf16[2048,2048]{1,0:T(8,128)(2,1)} %param.7), kind=kOutput, calls=%fused_computation.4 | convolution fusion | flops 8589934592 | bytes 20971520 | tf_op jit(solution)/shard_map/dot_general | solution.py:18
  193.6 0.0 reduce-scatter.5.cloned.1.call-update
  193.6 0.0 reduce-scatter.3.cloned.1.call-start
  193.6 67.3 %all-gather.5.cloned.1.call-done = bf16[1024,2048]{1,0:T(8,128)(2,1)} async-done(((bf16[256,2048]{1,0:T(8,128)(2,1)}), bf16[1024,2048]{1,0:T(8,128)(2,1)}) %all-gather.5.cloned.1.call-update) | async-done | bytes 4194320 | tf_op jit(solution)/shard_map/all_gather | solution.py:12
  260.9 14.9 %fusion = f32[1024,2048]{1,0:T(8,128)} fusion(bf16[1024,2048]{1,0:T(8,128)(2,1)} %all-gather.5.cloned.1.call-done, bf16[2048,2048]{1,0:T(8,128)(2,1)} %param.6), kind=kOutput, calls=%fused_computation.3 | convolution fusion | flops 8589934592 | bytes 20971520 | tf_op jit(solution)/shard_map/dot_general | solution.py:18
  275.8 0.0 reduce-scatter.3.cloned.1.call-update
  275.8 0.0 all-gather.11.cloned.1.call-start
  275.9 57.9 %reduce-scatter.5.cloned.1.call-done = f32[256,2048]{1,0:T(8,128)} async-done(((f32[1024,2048]{1,0:T(8,128)}), f32[256,2048]{1,0:T(8,128)}) %reduce-scatter.5.cloned.1.call-update) | async-done | bytes 2097168 | tf_op jit(solution)/shard_map/reduce_scatter | solution.py:21
  333.8 2.7 multiply_convert_fusion
  336.5 0.0 all-gather.11.cloned.1.call-update
  336.6 0.0 all-gather.7.cloned.1.call-start
  336.6 71.5 %reduce-scatter.3.cloned.1.call-done = f32[256,2048]{1,0:T(8,128)} async-done(((f32[1024,2048]{1,0:T(8,128)}), f32[256,2048]{1,0:T(8,128)}) %reduce-scatter.3.cloned.1.call-update) | async-done | bytes 2097168 | tf_op jit(solution)/shard_map/reduce_scatter | solution.py:21
  408.1 1.8 multiply_convert_fusion.1
  409.9 0.7 collective-permute-start.1
  410.6 0.0 collective-permute-done.1
  410.6 0.0 copy-start.2
  410.6 1.0 copy-done.2
  411.6 0.0 all-gather.7.cloned.1.call-update
  411.6 50.1 %all-gather.11.cloned.1.call-done = bf16[1024,2048]{1,0:T(8,128)(2,1)} async-done(((bf16[256,2048]{1,0:T(8,128)(2,1)}), bf16[1024,2048]{1,0:T(8,128)(2,1)}) %all-gather.11.cloned.1.call-update) | async-done | bytes 4194320 | tf_op jit(solution)/shard_map/all_gather | solution.py:31
  461.7 85.2 %all-gather.7.cloned.1.call-done = bf16[1024,2048]{1,0:T(8,128)(2,1)} async-done(((bf16[256,2048]{1,0:T(8,128)(2,1)}), bf16[1024,2048]{1,0:T(8,128)(2,1)}) %all-gather.7.cloned.1.call-update) | async-done | bytes 4194320 | tf_op jit(solution)/shard_map/all_gather | solution.py:12
  546.9 15.4 %convolution_multiply_fusion = f32[2048,2048]{1,0:T(8,128)} fusion(bf16[1024,2048]{1,0:T(8,128)(2,1)} %all-gather.7.cloned.1.call-done, bf16[1024,2048]{1,0:T(8,128)(2,1)} %all-gather.11.cloned.1.call-done), kind=kOutput, calls=%fused_computation | convolution fusion | flops 8594128896 | bytes 25165824 | tf_op jit(solution)/shard_map/dot_general | solution.py:33
Async XLA Ops:
  6.5 172.5 %all-gather.9.cloned.1.call-start = ((), (), s32[]{:S(2)}) async-start(), calls=%async_computation.5 | async-start | bytes 5242880 | tf_op jit(solution)/shard_map/all_gather | solution.py:12
  6.5 1.9 collective-permute-start.2
  8.4 1.0 copy-start
  9.4 251.5 %all-gather.5.cloned.1.call-start = ((), (), s32[]{:S(2)}) async-start(), calls=%async_computation.2 | async-start | bytes 5242880 | tf_op jit(solution)/shard_map/all_gather | solution.py:12
  9.5 1.9 collective-permute-start
  11.4 1.0 copy-start.1
  12.3 321.4 %reduce-scatter.5.cloned.1.call-start = ((), (), s32[]{:S(2)}) async-start(), calls=%async_computation.6 | async-start | bytes 10485760 | tf_op jit(solution)/shard_map/reduce_scatter | solution.py:21
  193.6 214.5 %reduce-scatter.3.cloned.1.call-start = ((), (), s32[]{:S(2)}) async-start(), calls=%async_computation.3 | async-start | bytes 10485760 | tf_op jit(solution)/shard_map/reduce_scatter | solution.py:21
  275.8 185.9 %all-gather.11.cloned.1.call-start = ((), (), s32[]{:S(2)}) async-start(), calls=%async_computation.7 | async-start | bytes 5242880 | tf_op jit(solution)/shard_map/all_gather | solution.py:31
  336.6 210.3 %all-gather.7.cloned.1.call-start = ((), (), s32[]{:S(2)}) async-start(), calls=%async_computation.4 | async-start | bytes 5242880 | tf_op jit(solution)/shard_map/all_gather | solution.py:12
  409.9 0.7 collective-permute-start.1
  410.6 1.0 copy-start.2
Sparse Core Ops, SparseCore 0:
  9.5 169.4 all-gather.8
  180.6 80.2 all-gather.4
  263.5 70.2 reduce-scatter.4
  336.4 71.6 reduce-scatter.2
  409.5 52.1 all-gather.10
  463.1 83.6 all-gather.6

commit v2 on v1

--- a/solution.py
+++ b/solution.py
@@ -1,6 +1,8 @@
 import jax
 import jax.numpy as jnp
 from jax import lax
+from jax.experimental import pallas as pl
+from jax.experimental.pallas import tpu as pltpu
 from jax.sharding import PartitionSpec as P
 
 
@@ -21,15 +23,304 @@
     return lax.psum_scatter(partial, "tok", scatter_dimension=0, tiled=True)
 
 
-def on_device(activations, gradients, input_basis, output_basis):
-    tok_rows = activations.shape[0]
+MESH = pl.DeviceIdType.MESH
+SUBS = 2
+
+
+def relay_kernel(
+    acts, grads, u_in, u_out, every_in, every_out, line,
+    xg, u, p, got_core, got_x, sq,
+    u_sem, line_send, line_recv, xg_send, xg_recv,
+    core_send, core_recv, x_send, x_recv, out_send, out_recv,
+):
+    t, z = lax.axis_index("tok"), lax.axis_index("basis")
+    n_tok, n_z = lax.axis_size("tok"), lax.axis_size("basis")
+    rows, cols = acts.shape
+    sub = rows // SUBS
+    core, chip = lax.rem(t, 2), lax.div(t, 2)
+    core_peer, x_peer = t + 1 - 2 * core, lax.rem(t + 2, n_tok)
+
+    barrier = pltpu.get_barrier_semaphore()
+    for k in range(1, n_tok):
+        pl.semaphore_signal(
+            barrier, inc=1, device_id={"tok": lax.rem(t + k, n_tok)}, device_id_type=MESH
+        )
+
+    @pl.when(z > 0)
+    def _():
+        pl.semaphore_signal(barrier, inc=1, device_id={"basis": z - 1}, device_id_type=MESH)
+
+    @pl.when(z < n_z - 1)
+    def _():
+        pl.semaphore_signal(barrier, inc=1, device_id={"basis": z + 1}, device_id_type=MESH)
+
+    @pl.when((z > 0) & (z < n_z - 1))
+    def _():
+        pl.semaphore_wait(barrier, n_tok + 1)
+
+    @pl.when((z == 0) | (z == n_z - 1))
+    def _():
+        pl.semaphore_wait(barrier, n_tok)
+
+    def part(s):
+        return pl.ds(s * sub, sub)
+
+    own = (acts, grads, sq.at[0])
+
+    def landing(a, src, s):
+        return every_in.at[src, part(s)] if a == 2 else xg.at[a, src, part(s)]
+
+    def line_copy(a, f, s, way, source):
+        return pltpu.make_async_remote_copy(
+            src_ref=source, dst_ref=line.at[a, f, part(s)],
+            send_sem=line_send.at[a, f, s, way], recv_sem=line_recv.at[a, f, s],
+            device_id={"basis": z + 1 if way else z - 1}, device_id_type=MESH,
+        )
+
+    def plane_copy(a, f, s, source):
+        return pltpu.make_async_remote_copy(
+            src_ref=source, dst_ref=landing(a, t, s),
+            send_sem=xg_send.at[a, f, s], recv_sem=xg_recv.at[a, t, s],
+            device_id={"tok": f}, device_id_type=MESH,
+        )
+
+    def to_plane(a, f, s, source):
+        @pl.when(t == f)
+        def _():
+            pltpu.make_async_copy(source, landing(a, t, s), xg_recv.at[a, t, s]).start()
+
+        @pl.when(t != f)
+        def _():
+            plane_copy(a, f, s, source).start()
+
+    def send_own(a, s):
+        source = own[a].at[part(s)]
+
+        @pl.when(z < n_z - 1)
+        def _():
+            line_copy(a, z, s, 1, source).start()
+
+        @pl.when(z > 0)
+        def _():
+            line_copy(a, z, s, 0, source).start()
+
+        to_plane(a, z, s, source)
+
+    def relay(a, d):
+        for s in range(SUBS):
+            @pl.when(z - d >= 0)
+            def _():
+                f = z - d
+                block = line.at[a, f, part(s)]
+                line_copy(a, f, s, 1, block).wait_recv()
+
+                @pl.when(z < n_z - 1)
+                def _():
+                    line_copy(a, f, s, 1, block).start()
+
+                to_plane(a, f, s, block)
+
+            @pl.when(z + d < n_z)
+            def _():
+                f = z + d
+                block = line.at[a, f, part(s)]
+                line_copy(a, f, s, 0, block).wait_recv()
+
+                @pl.when(z > 0)
+                def _():
+                    line_copy(a, f, s, 0, block).start()
+
+                to_plane(a, f, s, block)
+
+    def arrived(a, src):
+        for s in range(SUBS):
+            pltpu.make_async_copy(
+                landing(a, src, s), landing(a, src, s), xg_recv.at[a, src, s]
+            ).wait()
+
+    def sent(a):
+        for s in range(SUBS):
+            for f in range(n_z):
+                source = line.at[a, f, part(s)]
+
+                @pl.when((f <= z) & (z < n_z - 1))
+                def _():
+                    line_copy(a, f, s, 1, source).wait_send()
+
+                @pl.when((f >= z) & (z > 0))
+                def _():
+                    line_copy(a, f, s, 0, source).wait_send()
+
+                @pl.when(t != f)
+                def _():
+                    plane_copy(a, f, s, source).wait_send()
+
+    def load_basis(a):
+        return pltpu.make_async_copy((u_in, u_out)[a], u, u_sem.at[a])
+
+    def core_copy(a, c, s):
+        return pltpu.make_async_remote_copy(
+            src_ref=p.at[a, 2 * c + 1 - core, part(s)], dst_ref=got_core.at[a, c, part(s)],
+            send_sem=core_send.at[a, c, s], recv_sem=core_recv.at[a, c, s],
+            device_id={"tok": core_peer}, device_id_type=MESH,
+        )
+
+    def x_copy(a, s):
+        return pltpu.make_async_remote_copy(
+            src_ref=p.at[a, x_peer, part(s)], dst_ref=got_x.at[a, part(s)],
+            send_sem=x_send.at[a, s], recv_sem=x_recv.at[a, s],
+            device_id={"tok": x_peer}, device_id_type=MESH,
+        )
+
+    step = 32
+
+    def project(a, tb):
+        def body(j, _):
+            at = pl.ds(pl.multiple_of(j * 512, 512), 512)
+            p[a, tb, :, at] = jnp.dot(xg[a, tb], u[:, at], preferred_element_type=jnp.float32)
+            return 0
+
+        lax.fori_loop(0, cols // 512, body, 0)
+
+    def add_core(a, c, s):
+        core_copy(a, c, s).wait_recv()
+
+        def body(i, _):
+            at = pl.ds(pl.multiple_of(s * sub + i * step, step), step)
+            p[a, 2 * c + core, at, :] += got_core[a, c, at, :]
+            return 0
+
+        lax.fori_loop(0, sub // step, body, 0)
+
+    def partials(a):
+        load_basis(a).wait()
+        for src in range(n_tok):
+            arrived(a, src)
+        for c in (1 - chip, chip):
+            project(a, 2 * c + 1 - core)
+            for s in range(SUBS):
+                core_copy(a, c, s).start()
+        project(a, x_peer)
+        for s in range(SUBS):
+            add_core(a, 1 - chip, s)
+            x_copy(a, s).start()
+        project(a, t)
+        if a == 0:
+            load_basis(1).start()
+        for s in range(SUBS):
+            add_core(a, chip, s)
+
+    def square(a, s):
+        x_copy(a, s).wait_recv()
+
+        def body(i, _):
+            at = pl.ds(pl.multiple_of(s * sub + i * step, step), step)
+            total = p[a, t, at, :] + got_x[a, at, :]
+            sq[a, at, :] = (total * total).astype(sq.dtype)
+            return 0
+
+        lax.fori_loop(0, sub // step, body, 0)
+
+    def out_copy(k, s):
+        return pltpu.make_async_remote_copy(
+            src_ref=sq.at[1, part(s)], dst_ref=every_out.at[t, part(s)],
+            send_sem=out_send.at[k, s], recv_sem=out_recv.at[t, s],
+            device_id={"tok": lax.rem(t + k, n_tok)}, device_id_type=MESH,
+        )
+
+    def own_out(s):
+        return pltpu.make_async_copy(
+            sq.at[1, part(s)], every_out.at[t, part(s)], out_send.at[0, s]
+        )
+
+    load_basis(0).start()
+    for s in range(SUBS):
+        send_own(0, s)
+    for d in range(1, n_z):
+        relay(0, d)
+    for s in range(SUBS):
+        send_own(1, s)
+    partials(0)
+    for d in range(1, n_z):
+        relay(1, d)
+    for s in range(SUBS):
+        square(0, s)
+        send_own(2, s)
+    partials(1)
+    for d in range(1, n_z - 1):
+        relay(2, d)
+    for s in range(SUBS):
+        square(1, s)
+        for k in (2, 1, 3):
+            out_copy(k, s).start()
+        own_out(s).start()
+    relay(2, n_z - 1)
+    for s in range(SUBS):
+        own_out(s).wait()
+        for k in range(1, n_tok):
+            out_copy(k, s).wait_send()
+            src = lax.rem(t + k, n_tok)
+            dst = every_out.at[src, part(s)]
+            pltpu.make_async_copy(dst, dst, out_recv.at[src, s]).wait()
+        for a in range(2):
+            x_copy(a, s).wait_send()
+            for c in (1 - chip, chip):
+                core_copy(a, c, s).wait_send()
+    for src in range(n_tok):
+        arrived(2, src)
+    for a in range(3):
+        sent(a)
+
+
+def relayed(activations, gradients, input_basis, output_basis):
+    n_tok, n_z = lax.axis_size("tok"), lax.axis_size("basis")
+    rows, cols = activations.shape
+    every = jax.ShapeDtypeStruct((n_tok, rows, cols), jnp.bfloat16)
+    dma = pltpu.SemaphoreType.DMA
+    every_in, every_out, _ = pl.pallas_call(
+        relay_kernel,
+        out_shape=(every, every, jax.ShapeDtypeStruct((3, n_z, rows, cols), jnp.bfloat16)),
+        in_specs=[pl.BlockSpec(memory_space=pl.ANY)] * 4,
+        out_specs=(pl.BlockSpec(memory_space=pl.ANY),) * 3,
+        scratch_shapes=[
+            pltpu.VMEM((2, n_tok, rows, cols), jnp.bfloat16),
+            pltpu.VMEM(input_basis.shape, jnp.bfloat16),
+            pltpu.VMEM((2, n_tok, rows, cols), jnp.float32),
+            pltpu.VMEM((2, 2, rows, cols), jnp.float32),
+            pltpu.VMEM((2, rows, cols), jnp.float32),
+            pltpu.VMEM((2, rows, cols), jnp.bfloat16),
+            dma((2,)),
+            dma((3, n_z, SUBS, 2)), dma((3, n_z, SUBS)),
+            dma((3, n_z, SUBS)), dma((3, n_tok, SUBS)),
+            dma((2, 2, SUBS)), dma((2, 2, SUBS)),
+            dma((2, SUBS)), dma((2, SUBS)),
+            dma((n_tok, SUBS)), dma((n_tok, SUBS)),
+        ],
+        compiler_params=pltpu.CompilerParams(
+            collective_id=0, has_side_effects=True, vmem_limit_bytes=60 * 2**20
+        ),
+        cost_estimate=pl.CostEstimate(
+            flops=4 * n_tok * rows * input_basis.size, bytes_accessed=2**26, transcendentals=0
+        ),
+    )(activations, gradients, input_basis, output_basis)
+    return every_in.reshape(-1, cols), every_out.reshape(-1, cols)
+
+
+def gathered(activations, gradients, input_basis, output_basis):
     projected_in = project(activations, input_basis)
     squared_in = (projected_in * projected_in).astype(jnp.bfloat16)
     projected_out = project(gradients, output_basis)
     squared_out = (projected_out * projected_out).astype(jnp.bfloat16)
-    every_in = all_tokens_of_own_block(squared_in)
-    every_out = lax.all_gather(squared_out, "tok", axis=0, tiled=True)
-    total_tokens = tok_rows * lax.axis_size("tok")
+    return all_tokens_of_own_block(squared_in), lax.all_gather(squared_out, "tok", axis=0, tiled=True)
+
+
+def on_device(activations, gradients, input_basis, output_basis):
+    rows, cols = activations.shape
+    n_tok, n_z = lax.axis_size("tok"), lax.axis_size("basis")
+    small = rows * cols <= 2**19 and rows % 64 == 0 and cols % 512 == 0
+    plan = relayed if n_tok == n_z == 4 and small else gathered
+    every_in, every_out = plan(activations, gradients, input_basis, output_basis)
+    total_tokens = rows * n_tok
     summed = lax.dot_general(
         every_in, every_out, (((0,), (0,)), ((), ())), preferred_element_type=jnp.float32
     )

time: 569 us -> 326 us (0.57)
  waiting for transfers between devices: 499 us -> 0 us
  Pallas kernels: 0 us -> 310 us
  matrix products: 44.8 us -> 15.4 us
  between operations: 13.5 us -> 0.01 us
    all_gather x4 -> x0, waiting for transfers between devices: 369 us -> none  [the longest x3 319 us: all_tokens_of_own_block(): return lax.all_gather(swapped, 'basis', axis=0, tiled=True)]
    pallas_call x0 -> x1, Pallas kernels: none -> 310 us  [relayed(): pl.pallas_call(relay_kernel, out_shape=(every, every, jax.ShapeDtypeStruc...]
    reduce_scatter x2 -> x0, waiting for transfers between devices: 129 us -> none  [project(): return lax.psum_scatter(partial, 'tok', scatter_dimension=0, tiled=True)]
    dot_general x2 -> x0, matrix products: 29.4 us -> none  [project(): jnp.dot(all_tokens_of_own_block(block), basis_block, preferred_element_ty...]
  transfers between devices with their start and end apart: 9 -> 0, of which waited for: 6 -> 0; matrix products, arithmetic and copies ran while one was open for 6% -> 0% of each run, Pallas kernels for 0% -> 0%
where the time goes in v2:
time: 326 us; the launch traced here: 325 us
  Pallas kernels  310 us (95%)
  matrix products  15.4 us (5%)
    pallas_call x1, Pallas kernels, relayed(): pl.pallas_call(relay_kernel, out_shape=(every, every, jax.ShapeDtypeStruc...  310 us
    dot_general x1, matrix products, on_device(): lax.dot_general(every_in, every_out, (((0,), (0,)), ((), ())), preferred_...  15.4 us

profile of v2, /device:TPU:0, one launch (start us, length us, event | category | flops | bytes accessed | tf_op | source)
XLA Modules:
  0.0 325.3 jit_solution(2848153531613507994)
XLA Ops:
  0.0 309.9 %shard_map.46 = (bf16[4,256,2048]{2,1,0:T(8,128)(2,1)}, bf16[4,256,2048]{2,1,0:T(8,128)(2,1)}, bf16[3,4,256,2048]{3,2,1,0:T(8,128)(2,1)}) custom-call(bf16[256,2048]{1,0:T(8,128)(2,1)} %acts.1, bf16[256,2048]{1,0:T(8,128)(2,1)} %grads.1, bf16[2048,2048]{1,0:T(8,128)(2,1)} %u_in.1, bf16[2048,2048]{1,0:T(8,128)(2,1)} %u_out.1), custom_call_target="tpu_custom_call" | custom-call | flops 17179869184 | bytes 67108864 | tf_op jit(solution)/shard_map/pallas_call | solution.py:280
  309.9 15.4 %bitcast_multiply_fusion = f32[2048,2048]{1,0:T(8,128)} fusion(bf16[4,256,2048]{2,1,0:T(8,128)(2,1)} %get-tuple-element.7, bf16[4,256,2048]{2,1,0:T(8,128)(2,1)} %get-tuple-element.8), kind=kOutput, calls=%fused_computation | convolution fusion | flops 8594128896 | bytes 25165824 | tf_op jit(solution)/shard_map/dot_general | solution.py:324

commit v3 on v2

--- a/solution.py
+++ b/solution.py
@@ -31,7 +31,7 @@
     acts, grads, u_in, u_out, every_in, every_out, line,
     xg, u, p, got_core, got_x, sq,
     u_sem, line_send, line_recv, xg_send, xg_recv,
-    core_send, core_recv, x_send, x_recv, out_send, out_recv,
+    pair_send, core_send, core_recv, x_send, x_recv, out_send, out_recv,
 ):
     t, z = lax.axis_index("tok"), lax.axis_index("basis")
     n_tok, n_z = lax.axis_size("tok"), lax.axis_size("basis")
@@ -84,76 +84,120 @@
             device_id={"tok": f}, device_id_type=MESH,
         )
 
+    def across(f):
+        return lax.div(f, 2) != chip
+
+    def same_parity(f):
+        return lax.rem(f, 2) == lax.rem(z, 2)
+
+    def hops_up(f, to):
+        last = n_z - 1
+        return (to <= last) & ~(across(f) & (to == last) & (lax.rem(f, 2) != last % 2))
+
+    def hops_down(f, to):
+        return (to >= 0) & ~(across(f) & (to == 0) & (lax.rem(f, 2) != 0))
+
+    def crosses(f):
+        return (t != f) & (~across(f) | same_parity(f))
+
     def to_plane(a, f, s, source):
         @pl.when(t == f)
         def _():
             pltpu.make_async_copy(source, landing(a, t, s), xg_recv.at[a, t, s]).start()
 
-        @pl.when(t != f)
+        @pl.when(crosses(f))
         def _():
             plane_copy(a, f, s, source).start()
 
     def send_own(a, s):
         source = own[a].at[part(s)]
 
-        @pl.when(z < n_z - 1)
+        @pl.when(hops_up(z, z + 1))
         def _():
             line_copy(a, z, s, 1, source).start()
 
-        @pl.when(z > 0)
+        @pl.when(hops_down(z, z - 1))
         def _():
             line_copy(a, z, s, 0, source).start()
 
         to_plane(a, z, s, source)
 
-    def relay(a, d):
-        for s in range(SUBS):
-            @pl.when(z - d >= 0)
+    def relay(a, s):
+        for d in range(1, n_z):
+            @pl.when((z - d >= 0) & hops_up(z - d, z))
             def _():
                 f = z - d
                 block = line.at[a, f, part(s)]
                 line_copy(a, f, s, 1, block).wait_recv()
 
-                @pl.when(z < n_z - 1)
+                @pl.when(hops_up(f, z + 1))
                 def _():
                     line_copy(a, f, s, 1, block).start()
 
                 to_plane(a, f, s, block)
 
-            @pl.when(z + d < n_z)
+            @pl.when((z + d < n_z) & hops_down(z + d, z))
             def _():
                 f = z + d
                 block = line.at[a, f, part(s)]
                 line_copy(a, f, s, 0, block).wait_recv()
 
-                @pl.when(z > 0)
+                @pl.when(hops_down(f, z - 1))
                 def _():
                     line_copy(a, f, s, 0, block).start()
 
                 to_plane(a, f, s, block)
 
-    def arrived(a, src):
-        for s in range(SUBS):
-            pltpu.make_async_copy(
-                landing(a, src, s), landing(a, src, s), xg_recv.at[a, src, s]
-            ).wait()
+    def landed(a, src, s):
+        pltpu.make_async_copy(
+            landing(a, src, s), landing(a, src, s), xg_recv.at[a, src, s]
+        ).wait()
+
+    def pair_copy(a, c, s):
+        src = 2 * (1 - chip) + c
+        return pltpu.make_async_remote_copy(
+            src_ref=landing(a, src, s), dst_ref=landing(a, src, s),
+            send_sem=pair_send.at[a, c, s], recv_sem=xg_recv.at[a, src, s],
+            device_id={"basis": z + 1 - 2 * lax.rem(z, 2)}, device_id_type=MESH,
+        )
+
+    def hand_on(a, s):
+        @pl.when(same_parity(t))
+        def _():
+            for c in range(2):
+                landed(a, 2 * (1 - chip) + c, s)
+                pair_copy(a, c, s).start()
+
+    def arrived(a, s):
+        landed(a, t, s)
+        landed(a, core_peer, s)
+
+        @pl.when(~same_parity(t))
+        def _():
+            for c in range(2):
+                landed(a, 2 * (1 - chip) + c, s)
 
     def sent(a):
         for s in range(SUBS):
             for f in range(n_z):
                 source = line.at[a, f, part(s)]
 
-                @pl.when((f <= z) & (z < n_z - 1))
+                @pl.when((f <= z) & hops_up(f, z + 1))
                 def _():
                     line_copy(a, f, s, 1, source).wait_send()
 
-                @pl.when((f >= z) & (z > 0))
+                @pl.when((f >= z) & hops_down(f, z - 1))
                 def _():
                     line_copy(a, f, s, 0, source).wait_send()
 
-                @pl.when(t != f)
+                @pl.when(crosses(f))
                 def _():
                     plane_copy(a, f, s, source).wait_send()
+
+            @pl.when(same_parity(t))
+            def _():
+                for c in range(2):
+                    pair_copy(a, c, s).wait_send()
 
     def load_basis(a):
         return pltpu.make_async_copy((u_in, u_out)[a], u, u_sem.at[a])
@@ -174,10 +218,12 @@
 
     step = 32
 
-    def project(a, tb):
+    def project(a, s):
         def body(j, _):
             at = pl.ds(pl.multiple_of(j * 512, 512), 512)
-            p[a, tb, :, at] = jnp.dot(xg[a, tb], u[:, at], preferred_element_type=jnp.float32)
+            left = xg[a, :, part(s), :].reshape(n_tok * sub, cols)
+            product = jnp.dot(left, u[:, at], preferred_element_type=jnp.float32)
+            p[a, :, part(s), at] = product.reshape(n_tok, sub, 512)
             return 0
 
         lax.fori_loop(0, cols // 512, body, 0)
@@ -192,23 +238,14 @@
 
         lax.fori_loop(0, sub // step, body, 0)
 
-    def partials(a):
-        load_basis(a).wait()
-        for src in range(n_tok):
-            arrived(a, src)
+    def partials(a, s):
+        arrived(a, s)
+        project(a, s)
         for c in (1 - chip, chip):
-            project(a, 2 * c + 1 - core)
-            for s in range(SUBS):
-                core_copy(a, c, s).start()
-        project(a, x_peer)
-        for s in range(SUBS):
-            add_core(a, 1 - chip, s)
-            x_copy(a, s).start()
-        project(a, t)
-        if a == 0:
-            load_basis(1).start()
-        for s in range(SUBS):
-            add_core(a, chip, s)
+            core_copy(a, c, s).start()
+        add_core(a, 1 - chip, s)
+        x_copy(a, s).start()
+        add_core(a, chip, s)
 
     def square(a, s):
         x_copy(a, s).wait_recv()
@@ -233,28 +270,42 @@
             sq.at[1, part(s)], every_out.at[t, part(s)], out_send.at[0, s]
         )
 
-    load_basis(0).start()
-    for s in range(SUBS):
-        send_own(0, s)
-    for d in range(1, n_z):
-        relay(0, d)
-    for s in range(SUBS):
-        send_own(1, s)
-    partials(0)
-    for d in range(1, n_z):
-        relay(1, d)
-    for s in range(SUBS):
-        square(0, s)
-        send_own(2, s)
-    partials(1)
-    for d in range(1, n_z - 1):
-        relay(2, d)
-    for s in range(SUBS):
+    def finish_out(s):
         square(1, s)
         for k in (2, 1, 3):
             out_copy(k, s).start()
         own_out(s).start()
-    relay(2, n_z - 1)
+
+    load_basis(0).start()
+    send_own(0, 0)
+    relay(0, 0)
+    send_own(0, 1)
+    hand_on(0, 0)
+    load_basis(0).wait()
+    partials(0, 0)
+    relay(0, 1)
+    send_own(1, 0)
+    hand_on(0, 1)
+    partials(0, 1)
+    load_basis(1).start()
+    relay(1, 0)
+    send_own(1, 1)
+    hand_on(1, 0)
+    load_basis(1).wait()
+    partials(1, 0)
+    relay(1, 1)
+    square(0, 0)
+    send_own(2, 0)
+    hand_on(1, 1)
+    square(0, 1)
+    send_own(2, 1)
+    partials(1, 1)
+    relay(2, 0)
+    hand_on(2, 0)
+    finish_out(0)
+    relay(2, 1)
+    hand_on(2, 1)
+    finish_out(1)
     for s in range(SUBS):
         own_out(s).wait()
         for k in range(1, n_tok):
@@ -266,8 +317,7 @@
             x_copy(a, s).wait_send()
             for c in (1 - chip, chip):
                 core_copy(a, c, s).wait_send()
-    for src in range(n_tok):
-        arrived(2, src)
+        arrived(2, s)
     for a in range(3):
         sent(a)
 
@@ -292,7 +342,7 @@
             dma((2,)),
             dma((3, n_z, SUBS, 2)), dma((3, n_z, SUBS)),
             dma((3, n_z, SUBS)), dma((3, n_tok, SUBS)),
-            dma((2, 2, SUBS)), dma((2, 2, SUBS)),
+            dma((3, 2, SUBS)), dma((2, 2, SUBS)), dma((2, 2, SUBS)),
             dma((2, SUBS)), dma((2, SUBS)),
             dma((n_tok, SUBS)), dma((n_tok, SUBS)),
         ],

time: 326 us -> 326 us (level)
  no operation moved by 1% of the time
where the time goes in v3:
time: 326 us; the launch traced here: 324 us
  Pallas kernels  309 us (95%)
  matrix products  15.4 us (5%)
    pallas_call x1, Pallas kernels, relayed(): pl.pallas_call(relay_kernel, out_shape=(every, every, jax.ShapeDtypeStruc...  309 us
    dot_general x1, matrix products, on_device(): lax.dot_general(every_in, every_out, (((0,), (0,)), ((), ())), preferred_...  15.4 us

profile of v3, /device:TPU:0, one launch (start us, length us, event | category | flops | bytes accessed | tf_op | source)
XLA Modules:
  0.0 323.9 jit_solution(13932129331395960843)
XLA Ops:
  0.0 308.5 %shard_map.46 = (bf16[4,256,2048]{2,1,0:T(8,128)(2,1)}, bf16[4,256,2048]{2,1,0:T(8,128)(2,1)}, bf16[3,4,256,2048]{3,2,1,0:T(8,128)(2,1)}) custom-call(bf16[256,2048]{1,0:T(8,128)(2,1)} %acts.1, bf16[256,2048]{1,0:T(8,128)(2,1)} %grads.1, bf16[2048,2048]{1,0:T(8,128)(2,1)} %u_in.1, bf16[2048,2048]{1,0:T(8,128)(2,1)} %u_out.1), custom_call_target="tpu_custom_call" | custom-call | flops 17179869184 | bytes 67108864 | tf_op jit(solution)/shard_map/pallas_call | solution.py:330
  308.5 15.4 %bitcast_multiply_fusion = f32[2048,2048]{1,0:T(8,128)} fusion(bf16[4,256,2048]{2,1,0:T(8,128)(2,1)} %get-tuple-element.7, bf16[4,256,2048]{2,1,0:T(8,128)(2,1)} %get-tuple-element.8), kind=kOutput, calls=%fused_computation | convolution fusion | flops 8594128896 | bytes 25165824 | tf_op jit(solution)/shard_map/dot_general | solution.py:374

commit v4 on v3

--- a/solution.py
+++ b/solution.py
@@ -122,31 +122,30 @@
 
         to_plane(a, z, s, source)
 
-    def relay(a, s):
-        for d in range(1, n_z):
-            @pl.when((z - d >= 0) & hops_up(z - d, z))
+    def relay(a, s, d):
+        @pl.when((z - d >= 0) & hops_up(z - d, z))
+        def _():
+            f = z - d
+            block = line.at[a, f, part(s)]
+            line_copy(a, f, s, 1, block).wait_recv()
+
+            @pl.when(hops_up(f, z + 1))
             def _():
-                f = z - d
-                block = line.at[a, f, part(s)]
-                line_copy(a, f, s, 1, block).wait_recv()
-
-                @pl.when(hops_up(f, z + 1))
-                def _():
-                    line_copy(a, f, s, 1, block).start()
-
-                to_plane(a, f, s, block)
-
-            @pl.when((z + d < n_z) & hops_down(z + d, z))
+                line_copy(a, f, s, 1, block).start()
+
+            to_plane(a, f, s, block)
+
+        @pl.when((z + d < n_z) & hops_down(z + d, z))
+        def _():
+            f = z + d
+            block = line.at[a, f, part(s)]
+            line_copy(a, f, s, 0, block).wait_recv()
+
+            @pl.when(hops_down(f, z - 1))
             def _():
-                f = z + d
-                block = line.at[a, f, part(s)]
-                line_copy(a, f, s, 0, block).wait_recv()
-
-                @pl.when(hops_down(f, z - 1))
-                def _():
-                    line_copy(a, f, s, 0, block).start()
-
-                to_plane(a, f, s, block)
+                line_copy(a, f, s, 0, block).start()
+
+            to_plane(a, f, s, block)
 
     def landed(a, src, s):
         pltpu.make_async_copy(
@@ -238,11 +237,13 @@
 
         lax.fori_loop(0, sub // step, body, 0)
 
-    def partials(a, s):
+    def start_sums(a, s):
         arrived(a, s)
         project(a, s)
         for c in (1 - chip, chip):
             core_copy(a, c, s).start()
+
+    def finish_sums(a, s):
         add_core(a, 1 - chip, s)
         x_copy(a, s).start()
         add_core(a, chip, s)
@@ -276,36 +277,46 @@
             out_copy(k, s).start()
         own_out(s).start()
 
+    def advance(before, now):
+        hand_on(*before)
+        relay(*now, 1)
+        if now == (0, 1):
+            send_own(1, 0)
+            load_basis(0).wait()
+        elif now == (1, 0):
+            send_own(1, 1)
+        elif now == (1, 1):
+            square(0, 0)
+            send_own(2, 0)
+            load_basis(1).wait()
+        elif now == (2, 0):
+            square(0, 1)
+            send_own(2, 1)
+        relay(*now, 2)
+        if before[0] < 2:
+            start_sums(*before)
+        if before == (0, 1):
+            load_basis(1).start()
+        relay(*now, 3)
+        if before[0] < 2:
+            finish_sums(*before)
+
     load_basis(0).start()
     send_own(0, 0)
-    relay(0, 0)
     send_own(0, 1)
-    hand_on(0, 0)
-    load_basis(0).wait()
-    partials(0, 0)
-    relay(0, 1)
-    send_own(1, 0)
-    hand_on(0, 1)
-    partials(0, 1)
-    load_basis(1).start()
-    relay(1, 0)
-    send_own(1, 1)
-    hand_on(1, 0)
-    load_basis(1).wait()
-    partials(1, 0)
-    relay(1, 1)
-    square(0, 0)
-    send_own(2, 0)
-    hand_on(1, 1)
-    square(0, 1)
-    send_own(2, 1)
-    partials(1, 1)
-    relay(2, 0)
+    for d in range(1, 4):
+        relay(0, 0, d)
+    advance((0, 0), (0, 1))
+    advance((0, 1), (1, 0))
+    advance((1, 0), (1, 1))
+    advance((1, 1), (2, 0))
     hand_on(2, 0)
+    relay(2, 1, 1)
     finish_out(0)
-    relay(2, 1)
+    relay(2, 1, 2)
+    finish_out(1)
+    relay(2, 1, 3)
     hand_on(2, 1)
-    finish_out(1)
     for s in range(SUBS):
         own_out(s).wait()
         for k in range(1, n_tok):

time: 326 us -> 279 us (0.86)
  Pallas kernels: 309 us -> 263 us
    pallas_call x1, Pallas kernels: 309 us -> 263 us  [relayed(): pl.pallas_call(relay_kernel, out_shape=(every, every, jax.ShapeDtypeStruc...]
where the time goes in v4:
time: 279 us; the launch traced here: 278 us
  Pallas kernels  263 us (94%)
  matrix products  15.4 us (6%)
    pallas_call x1, Pallas kernels, relayed(): pl.pallas_call(relay_kernel, out_shape=(every, every, jax.ShapeDtypeStruc...  263 us
    dot_general x1, matrix products, on_device(): lax.dot_general(every_in, every_out, (((0,), (0,)), ((), ())), preferred_...  15.4 us

profile of v4, /device:TPU:0, one launch (start us, length us, event | category | flops | bytes accessed | tf_op | source)
XLA Modules:
  0.0 278.4 jit_solution(8854774572508159360)
XLA Ops:
  0.0 263.0 %shard_map.46 = (bf16[4,256,2048]{2,1,0:T(8,128)(2,1)}, bf16[4,256,2048]{2,1,0:T(8,128)(2,1)}, bf16[3,4,256,2048]{3,2,1,0:T(8,128)(2,1)}) custom-call(bf16[256,2048]{1,0:T(8,128)(2,1)} %acts.1, bf16[256,2048]{1,0:T(8,128)(2,1)} %grads.1, bf16[2048,2048]{1,0:T(8,128)(2,1)} %u_in.1, bf16[2048,2048]{1,0:T(8,128)(2,1)} %u_out.1), custom_call_target="tpu_custom_call" | custom-call | flops 17179869184 | bytes 67108864 | tf_op jit(solution)/shard_map/pallas_call | solution.py:341
  263.0 15.4 %bitcast_multiply_fusion = f32[2048,2048]{1,0:T(8,128)} fusion(bf16[4,256,2048]{2,1,0:T(8,128)(2,1)} %get-tuple-element.7, bf16[4,256,2048]{2,1,0:T(8,128)(2,1)} %get-tuple-element.8), kind=kOutput, calls=%fused_computation | convolution fusion | flops 8594128896 | bytes 25165824 | tf_op jit(solution)/shard_map/dot_general | solution.py:385

commit v5 on v4

--- a/solution.py
+++ b/solution.py
@@ -24,7 +24,7 @@
 
 
 MESH = pl.DeviceIdType.MESH
-SUBS = 2
+SUBS = 4
 
 
 def relay_kernel(
@@ -277,46 +277,36 @@
             out_copy(k, s).start()
         own_out(s).start()
 
-    def advance(before, now):
+    stages = [(a, s) for a in range(3) for s in range(SUBS)]
+    load_basis(0).start()
+    send_own(*stages[0])
+    send_own(*stages[1])
+    for d in (1, 2, 3):
+        relay(*stages[0], d)
+    for i in range(1, len(stages)):
+        before, now = stages[i - 1], stages[i]
         hand_on(*before)
         relay(*now, 1)
-        if now == (0, 1):
-            send_own(1, 0)
-            load_basis(0).wait()
-        elif now == (1, 0):
-            send_own(1, 1)
-        elif now == (1, 1):
-            square(0, 0)
-            send_own(2, 0)
-            load_basis(1).wait()
-        elif now == (2, 0):
-            square(0, 1)
-            send_own(2, 1)
+        if i + 1 < len(stages):
+            after = stages[i + 1]
+            if after[0] == 2:
+                square(0, after[1])
+            send_own(*after)
+        if now[0] == 2 and now[1] > 0:
+            finish_out(now[1] - 1)
         relay(*now, 2)
         if before[0] < 2:
+            if before[1] == 0:
+                load_basis(before[0]).wait()
             start_sums(*before)
-        if before == (0, 1):
-            load_basis(1).start()
+            if before == (0, SUBS - 1):
+                load_basis(1).start()
+        if i + 1 == len(stages):
+            finish_out(now[1])
         relay(*now, 3)
         if before[0] < 2:
             finish_sums(*before)
-
-    load_basis(0).start()
-    send_own(0, 0)
-    send_own(0, 1)
-    for d in range(1, 4):
-        relay(0, 0, d)
-    advance((0, 0), (0, 1))
-    advance((0, 1), (1, 0))
-    advance((1, 0), (1, 1))
-    advance((1, 1), (2, 0))
-    hand_on(2, 0)
-    relay(2, 1, 1)
-    finish_out(0)
-    relay(2, 1, 2)
-    finish_out(1)
-    relay(2, 1, 3)
-    hand_on(2, 1)
+    hand_on(*stages[-1])
     for s in range(SUBS):
         own_out(s).wait()
         for k in range(1, n_tok):

time: 279 us -> 264 us (0.946)
  Pallas kernels: 263 us -> 248 us
    pallas_call x1, Pallas kernels: 263 us -> 248 us  [relayed(): pl.pallas_call(relay_kernel, out_shape=(every, every, jax.ShapeDtypeStruc...]
where the time goes in v5:
time: 264 us; the launch traced here: 263 us
  Pallas kernels  248 us (94%)
  matrix products  15.4 us (6%)
    pallas_call x1, Pallas kernels, relayed(): pl.pallas_call(relay_kernel, out_shape=(every, every, jax.ShapeDtypeStruc...  248 us
    dot_general x1, matrix products, on_device(): lax.dot_general(every_in, every_out, (((0,), (0,)), ((), ())), preferred_...  15.4 us

profile of v5, /device:TPU:0, one launch (start us, length us, event | category | flops | bytes accessed | tf_op | source)
XLA Modules:
  0.0 263.4 jit_solution(13048179642706725299)
XLA Ops:
  0.0 248.0 %shard_map.46 = (bf16[4,256,2048]{2,1,0:T(8,128)(2,1)}, bf16[4,256,2048]{2,1,0:T(8,128)(2,1)}, bf16[3,4,256,2048]{3,2,1,0:T(8,128)(2,1)}) custom-call(bf16[256,2048]{1,0:T(8,128)(2,1)} %acts.1, bf16[256,2048]{1,0:T(8,128)(2,1)} %grads.1, bf16[2048,2048]{1,0:T(8,128)(2,1)} %u_in.1, bf16[2048,2048]{1,0:T(8,128)(2,1)} %u_out.1), custom_call_target="tpu_custom_call" | custom-call | flops 17179869184 | bytes 67108864 | tf_op jit(solution)/shard_map/pallas_call | solution.py:331
  248.0 15.4 %bitcast_multiply_fusion = f32[2048,2048]{1,0:T(8,128)} fusion(bf16[4,256,2048]{2,1,0:T(8,128)(2,1)} %get-tuple-element.7, bf16[4,256,2048]{2,1,0:T(8,128)(2,1)} %get-tuple-element.8), kind=kOutput, calls=%fused_computation | convolution fusion | flops 8594128896 | bytes 25165824 | tf_op jit(solution)/shard_map/dot_general | solution.py:375

commit v6 on v5

--- a/solution.py
+++ b/solution.py
@@ -285,8 +285,8 @@
         relay(*stages[0], d)
     for i in range(1, len(stages)):
         before, now = stages[i - 1], stages[i]
+        relay(*now, 1)
         hand_on(*before)
-        relay(*now, 1)
         if i + 1 < len(stages):
             after = stages[i + 1]
             if after[0] == 2:

time: 264 us -> 256 us (0.970)
  Pallas kernels: 248 us -> 241 us
    pallas_call x1, Pallas kernels: 248 us -> 241 us  [relayed(): pl.pallas_call(relay_kernel, out_shape=(every, every, jax.ShapeDtypeStruc...]
where the time goes in v6:
time: 256 us
  Pallas kernels  241 us (94%)
  matrix products  15.4 us (6%)
    pallas_call x1, Pallas kernels, relayed(): pl.pallas_call(relay_kernel, out_shape=(every, every, jax.ShapeDtypeStruc...  241 us
    dot_general x1, matrix products, on_device(): lax.dot_general(every_in, every_out, (((0,), (0,)), ((), ())), preferred_...  15.4 us

profile of v6, /device:TPU:0, one launch (start us, length us, event | category | flops | bytes accessed | tf_op | source)
XLA Modules:
  0.0 256.2 jit_solution(4625510820250400314)
XLA Ops:
  0.0 240.8 %shard_map.46 = (bf16[4,256,2048]{2,1,0:T(8,128)(2,1)}, bf16[4,256,2048]{2,1,0:T(8,128)(2,1)}, bf16[3,4,256,2048]{3,2,1,0:T(8,128)(2,1)}) custom-call(bf16[256,2048]{1,0:T(8,128)(2,1)} %acts.1, bf16[256,2048]{1,0:T(8,128)(2,1)} %grads.1, bf16[2048,2048]{1,0:T(8,128)(2,1)} %u_in.1, bf16[2048,2048]{1,0:T(8,128)(2,1)} %u_out.1), custom_call_target="tpu_custom_call" | custom-call | flops 17179869184 | bytes 67108864 | tf_op jit(solution)/shard_map/pallas_call | solution.py:331
  240.8 15.4 %bitcast_multiply_fusion = f32[2048,2048]{1,0:T(8,128)} fusion(bf16[4,256,2048]{2,1,0:T(8,128)(2,1)} %get-tuple-element.7, bf16[4,256,2048]{2,1,0:T(8,128)(2,1)} %get-tuple-element.8), kind=kOutput, calls=%fused_computation | convolution fusion | flops 8594128896 | bytes 25165824 | tf_op jit(solution)/shard_map/dot_general | solution.py:375
